TPU v7x, 32 devices: a whole 2x2x4 slice. The times are simulated.
32 devices in a mesh: groups: 2 (over x), seg: 16 (over z, y, core).
Axes of the slice: x: 2, y: 2, z: 4, core: 2. Of those that a mesh axis runs over, the one named last changes fastest.
Arguments:
- edge_env: float32 [32, 14, 4, 128, 128], P(('groups', 'seg')), parts along dimension 0, may hold values from -0.5 to 0.5
- start_vector: float32 [32, 2, 128, 512], P(('groups', 'seg')), parts along dimension 0, may hold values from -6 to 6
- mpo: float32 [112, 56], P('groups'), parts along dimension 0, may hold values from -0.75 to 0.75
- sector_map: int32 [14, 4], replicated, may hold values from 0 to 3
Outputs:
- new_vector: float32 [32, 2, 128, 512], P(('groups', 'seg')), parts along dimension 0
- grown_env: float32 [32, 14, 2, 128, 128], P(('groups', 'seg')), parts along dimension 0
- energy: float32 [32], P(('groups', 'seg')), parts along dimension 0
There are 2 independent parts, one for each index of `groups`. A program takes and returns all parts, laid end to end along the dimension named above; an argument that names none is the same for every part. Nothing has to cross between parts.
All inputs are finite; a program needn't handle non-finite values.
Results may differ from a plain program's by a relative error of at most 0.000082.
Values sent between devices are 32-bit elements; how exact they have to be, the bound alone decides.
A program may use at most 128 MiB of HBM per device.

v0:
```python
import jax
import jax.numpy as jnp
from jax import lax
from jax.experimental import pallas as pl
from jax.experimental.pallas import tpu as pltpu
from jax.sharding import PartitionSpec as P

epsilon = 1e-06
f32 = jnp.float32
bf16 = jnp.bfloat16


def split(value):
    high = value.astype(bf16)
    low = (value - high.astype(f32)).astype(bf16)
    return high, low


def dot(left, right):
    return lax.dot_general(left, right, (((1,), (0,)), ((), ())), preferred_element_type=f32)


def dot_t(left, right):
    return lax.dot_general(left, right, (((1,), (1,)), ((), ())), preferred_element_type=f32)


def total(value):
    return jnp.sum(jnp.sum(value, axis=0, keepdims=True), axis=1, keepdims=True)


def make_kernel(seg_count, w_dim, sectors, bond, phys):
    halves = sectors // 2
    rows = w_dim * phys
    krows = rows * 8
    entries = float(sectors * bond * phys * bond)

    def kernel(env, start, mpo, smap, fresh_out, grown_out, energy_out,
               lr, v1, w1, vh, vl, xs, yh1, yl1, yh2, yl2, mix3, vt, acc, g11, gx, g22,
               mine, theirs, send, recv, local):
        seg = lax.axis_index("seg")
        upper = seg // (seg_count // 2)
        offset = upper * halves
        other = lax.rem(seg + seg_count // 2, seg_count)
        peer = (lax.axis_index("groups"), other)

        barrier = pltpu.get_barrier_semaphore()
        pl.semaphore_signal(barrier, inc=1, device_id=peer, device_id_type=pl.DeviceIdType.MESH)
        pl.semaphore_wait(barrier, 1)

        def remote(src, dst, index):
            return pltpu.make_async_remote_copy(
                src_ref=src, dst_ref=dst, send_sem=send.at[index], recv_sem=recv.at[index],
                device_id=peer, device_id_type=pl.DeviceIdType.MESH)

        vec_copy = remote(start, v1.at[pl.ds(offset, halves)], 0)
        env_copy = [remote(env.at[:, halves - offset + t], lr.at[upper, t], 1 + t) for t in range(halves)]
        own_vec = pltpu.make_async_copy(start, v1.at[pl.ds(offset, halves)], local.at[0])
        own_env = [pltpu.make_async_copy(env.at[:, offset + t], lr.at[upper, t], local.at[1 + t]) for t in range(halves)]
        vec_copy.start()
        env_copy[0].start()
        own_vec.start()
        for copy in own_env:
            copy.start()

        spread = ((lax.broadcasted_iota(jnp.int32, (krows, rows), 0) >> 3)
                  == lax.broadcasted_iota(jnp.int32, (krows, rows), 1)).astype(f32).astype(bf16)
        eye = ((lax.broadcasted_iota(jnp.int32, (krows, krows), 0) & 7)
               == (lax.broadcasted_iota(jnp.int32, (krows, krows), 1) & 7))
        m_high, m_low = split(mpo[...].T)
        e_high = jnp.where(eye, dot_t(dot(spread, m_high).astype(bf16), spread), 0.0).astype(bf16)
        e_low = jnp.where(eye, dot_t(dot(spread, m_low).astype(bf16), spread), 0.0).astype(bf16)
        mix3[:, :] = jnp.concatenate([e_high, e_high, e_low], axis=1)

        own_vec.wait()
        for copy in own_env:
            copy.wait()
        vec_copy.wait()

        def scale_split(ref, divisor):
            for u in range(sectors):
                value = ref[u] / divisor
                ref[u] = value
                high, low = split(value)
                vh[u] = high
                vl[u] = low

        def turn(ref, place):
            for t in range(halves):
                for s in range(phys):
                    block = ref[offset + t, :, s * bond:(s + 1) * bond].T
                    high, low = split(block)
                    at = slice(place * bond, (place + 1) * bond)
                    vt[t, at, s * bond:(s + 1) * bond] = high
                    vt[t, at, (phys + s) * bond:(phys + s + 1) * bond] = high
                    vt[t, at, (2 * phys + s) * bond:(2 * phys + s + 1) * bond] = low

        def contract(t, y_high, y_low):
            def left(w, carry):
                high, low = split(lr[0, t, w])
                m = smap[w, offset + t]
                v_high = vh[m]
                v_low = vl[m]
                out = dot(jnp.concatenate([high, high, low], axis=1),
                          jnp.concatenate([v_high, v_low, v_high], axis=0))
                for s in range(phys):
                    xs[w * phys + s] = out[:, s * bond:(s + 1) * bond]
                return carry

            lax.fori_loop(0, w_dim, left, 0, unroll=2)

            def mix(j, carry):
                first = xs[:, pl.ds(j * 16, 8), :].reshape(krows, bond)
                second = xs[:, pl.ds(j * 16 + 8, 8), :].reshape(krows, bond)
                high, low = split(jnp.concatenate([first, second], axis=1))
                out = dot(mix3[...], jnp.concatenate([high, low, high], axis=0))
                both = jnp.concatenate([out[:, :bond].reshape(rows, 8, bond),
                                        out[:, bond:].reshape(rows, 8, bond)], axis=1)
                high, low = split(both)
                y_high[t, :, pl.ds(j * 16, 16), :] = high
                y_low[t, :, pl.ds(j * 16, 16), :] = low
                return carry

            lax.fori_loop(0, bond // 16, mix, 0)

        def right(t):
            acc[...] = jnp.zeros_like(acc)

            def step(w, carry):
                r_high, r_low = split(lr[1, t, w])
                high = yh1[t, pl.ds(w * phys, phys)].reshape(phys * bond, bond)
                low = yl1[t, pl.ds(w * phys, phys)].reshape(phys * bond, bond)
                acc[...] += dot_t(jnp.concatenate([high, high, low], axis=1),
                                  jnp.concatenate([r_high, r_low, r_high], axis=1))
                return carry

            lax.fori_loop(0, w_dim, step, 0, unroll=2)
            for s in range(phys):
                w1[offset + t, :, s * bond:(s + 1) * bond] = acc[s * bond:(s + 1) * bond, :]

        def stacked(y_high, y_low, t, w):
            high = y_high[t, pl.ds(w * phys, phys)].reshape(phys * bond, bond)
            low = y_low[t, pl.ds(w * phys, phys)].reshape(phys * bond, bond)
            return jnp.concatenate([high, low, high], axis=0)

        norm = epsilon + sum(total(v1[u] * v1[u]) for u in range(sectors)) / entries
        scale_split(v1, jnp.sqrt(norm))
        turn(v1, 0)

        env_copy[0].wait_send()
        for copy in env_copy[1:]:
            copy.start()
        w_copy = [remote(w1.at[offset + t], w1.at[offset + t], 1 + halves + t) for t in range(halves)]
        for t in range(halves):
            env_copy[t].wait_recv()
            contract(t, yh1, yl1)
            right(t)
            w_copy[t].start()
        for copy in env_copy[1:]:
            copy.wait_send()

        def grow_one(w, carry):
            for t in range(halves):
                g11[w, t] = dot(vt[t, :bond, :], stacked(yh1, yl1, t, w))
            return carry

        lax.fori_loop(0, w_dim, grow_one, 0)
        for copy in w_copy:
            copy.wait()

        r1 = sum(total(v1[u] * w1[u]) for u in range(sectors)) / entries
        square = 0.0
        for u in range(sectors):
            res = w1[u] - r1 * v1[u]
            w1[u] = res
            square = square + total(res * res)
        q = jnp.sqrt(square / entries + epsilon)
        scale_split(w1, q)
        for t in range(halves):
            contract(t, yh2, yl2)
        turn(w1, 1)

        mine[...] = jnp.zeros_like(mine)

        def grow_two(w, carry):
            for t in range(halves):
                out = dot(vt[t], stacked(yh2, yl2, t, w))
                gx[w, t] = out[:bond]
                g22[w, t] = out[bond:]
                prod = out[bond:] * lr[1, t, w]
                mine[...] += jnp.sum(prod.reshape(bond // 8, 8, bond), axis=0)
            return carry

        lax.fori_loop(0, w_dim, grow_two, 0)
        r_copy = remote(mine, theirs, 1 + 2 * halves)
        r_copy.start()

        def grow_three(w, carry):
            for t in range(halves):
                gx[w, t] += dot(vt[t, bond:, :], stacked(yh1, yl1, t, w))
            return carry

        lax.fori_loop(0, w_dim, grow_three, 0)
        r_copy.wait()
        r2 = total(mine[...] + theirs[...]) / entries
        g = 0.5 * (r1 - r2)
        root = jnp.sqrt(g * g + q * q)
        energy_out[...] = jnp.broadcast_to(0.5 * (r1 + r2) - root, energy_out.shape)
        x = root - g
        y = -q
        length = jnp.sqrt(x * x + y * y)
        x = x / length
        y = y / length
        for t in range(halves):
            fresh_out[t] = x * v1[offset + t] + y * w1[offset + t]
        scale = 1.0 / jnp.sqrt(f32(phys * bond))
        c11 = x * x * scale
        c12 = x * y * scale
        c22 = y * y * scale

        def finish(w, carry):
            for t in range(halves):
                grown_out[w, t] = c11 * g11[w, t] + c12 * gx[w, t] + c22 * g22[w, t]
            return carry

        lax.fori_loop(0, w_dim, finish, 0)

    return kernel


def shards(edge_env, start_vector, mpo, sector_map):
    _, w_dim, sectors, bond, _ = edge_env.shape
    phys = start_vector.shape[3] // bond
    halves = sectors // 2
    rows = w_dim * phys
    krows = rows * 8
    seg_count = lax.axis_size("seg")
    vmem = pl.BlockSpec(memory_space=pltpu.VMEM)
    hbm = pl.BlockSpec(memory_space=pl.ANY)
    smem = pl.BlockSpec(memory_space=pltpu.SMEM)
    wide = (sectors, bond, phys * bond)
    big = (halves, rows, bond, bond)
    env = (w_dim, halves, bond, bond)
    fresh, grown, energy = pl.pallas_call(
        make_kernel(seg_count, w_dim, sectors, bond, phys),
        out_shape=(
            jax.ShapeDtypeStruct((halves, bond, phys * bond), f32),
            jax.ShapeDtypeStruct(env, f32),
            jax.ShapeDtypeStruct((8, 128), f32),
        ),
        in_specs=[hbm, hbm, vmem, smem],
        out_specs=(vmem, vmem, vmem),
        scratch_shapes=[
            pltpu.VMEM((2, halves, w_dim, bond, bond), f32),
            pltpu.VMEM(wide, f32),
            pltpu.VMEM(wide, f32),
            pltpu.VMEM(wide, bf16),
            pltpu.VMEM(wide, bf16),
            pltpu.VMEM((rows, bond, bond), f32),
            pltpu.VMEM(big, bf16),
            pltpu.VMEM(big, bf16),
            pltpu.VMEM(big, bf16),
            pltpu.VMEM(big, bf16),
            pltpu.VMEM((krows, 3 * krows), bf16),
            pltpu.VMEM((halves, 2 * bond, 3 * phys * bond), bf16),
            pltpu.VMEM((phys * bond, bond), f32),
            pltpu.VMEM(env, f32),
            pltpu.VMEM(env, f32),
            pltpu.VMEM(env, f32),
            pltpu.VMEM((8, 128), f32),
            pltpu.VMEM((8, 128), f32),
            pltpu.SemaphoreType.DMA((2 + 2 * halves,)),
            pltpu.SemaphoreType.DMA((2 + 2 * halves,)),
            pltpu.SemaphoreType.DMA((1 + halves,)),
        ],
        compiler_params=pltpu.CompilerParams(
            collective_id=0, has_side_effects=True, vmem_limit_bytes=56 * 1024 * 1024),
    )(edge_env[0], start_vector[0], mpo, sector_map)
    return (fresh[None], grown[None], energy[0, :1])


def solution(mesh):
    placed = (
        P(("groups", "seg"), None, None, None, None),
        P(("groups", "seg"), None, None, None),
        P("groups", None),
        P(),
    )
    return jax.shard_map(
        shards,
        mesh=mesh,
        in_specs=placed,
        out_specs=(
            P(("groups", "seg"), None, None, None),
            P(("groups", "seg"), None, None, None, None),
            P(("groups", "seg")),
        ),
        check_vma=False,
    )
```

profile of v0, /device:TPU:8, one launch (start us, length us, event | category | flops | bytes accessed | tf_op | source)
XLA Modules:
  0.0 166.7 jit_solution(1809740867291584458)
XLA Ops:
  0.6 1.4 copy.7.smap
  2.0 158.7 %shard_map.67 = (f32[2,128,512]{2,1,0:T(8,128)}, f32[14,2,128,128]{3,2,1,0:T(8,128)}, f32[8,128]{1,0:T(8,128)}) custom-call(f32[14,4,128,128]{3,2,1,0:T(8,128)} %bitcast.5, f32[2,128,512]{2,1,0:T(8,128)} %bitcast.7, f32[56,56]{1,0:T(8,128)} %mpo.1, s32[14,4]{1,0:T(8,128)} %copy.7.smap), custom_call_target="tpu_custom_call" | custom-call | tf_op jit(solution)/shard_map/pallas_call | solution.py:243
  160.7 1.2 slice.3
  161.9 1.9 %copy.10 = f32[1,2,128,512]{3,2,1,0:T(8,128)} copy(f32[1,2,128,512]{3,2,1,0:T(8,128)} %bitcast.8) | data formatting | bytes 1048576
  163.7 2.9 %copy.11 = f32[1,14,2,128,128]{4,3,2,1,0:T(8,128)} copy(f32[1,14,2,128,128]{4,3,2,1,0:T(8,128)} %bitcast.6) | data formatting | bytes 3670016
where the time goes:
time: 167 us
  Pallas kernels  159 us (95%)
  local copies, waits for them, and re-layouts  7.34 us (4%)
    pallas_call x1, Pallas kernels, shards(): pl.pallas_call(make_kernel(seg_count, w_dim, sectors, bond, phys), out_sh...  159 us
    unnamed x3, local copies, waits for them, and re-layouts  6.16 us

commit v1 on v0

--- a/solution.py
+++ b/solution.py
@@ -97,7 +97,7 @@
         def contract(t, y_high, y_low):
             def left(w, carry):
                 high, low = split(lr[0, t, w])
-                m = smap[w, offset + t]
+                m = smap[offset + t, w]
                 v_high = vh[m]
                 v_low = vl[m]
                 out = dot(jnp.concatenate([high, high, low], axis=1),
@@ -106,7 +106,7 @@
                     xs[w * phys + s] = out[:, s * bond:(s + 1) * bond]
                 return carry
 
-            lax.fori_loop(0, w_dim, left, 0, unroll=2)
+            lax.fori_loop(0, w_dim, left, 0, unroll=7)
 
             def mix(j, carry):
                 first = xs[:, pl.ds(j * 16, 8), :].reshape(krows, bond)
@@ -120,50 +120,59 @@
                 y_low[t, :, pl.ds(j * 16, 16), :] = low
                 return carry
 
-            lax.fori_loop(0, bond // 16, mix, 0)
+            lax.fori_loop(0, bond // 16, mix, 0, unroll=4)
 
         def right(t):
             acc[...] = jnp.zeros_like(acc)
 
-            def step(w, carry):
-                r_high, r_low = split(lr[1, t, w])
-                high = yh1[t, pl.ds(w * phys, phys)].reshape(phys * bond, bond)
-                low = yl1[t, pl.ds(w * phys, phys)].reshape(phys * bond, bond)
-                acc[...] += dot_t(jnp.concatenate([high, high, low], axis=1),
-                                  jnp.concatenate([r_high, r_low, r_high], axis=1))
+            def step(i, carry):
+                ys, rs = [], []
+                for j in range(2):
+                    w = 2 * i + j
+                    r_high, r_low = split(lr[1, t, w])
+                    high = yh1[t, pl.ds(w * phys, phys)].reshape(phys * bond, bond)
+                    low = yl1[t, pl.ds(w * phys, phys)].reshape(phys * bond, bond)
+                    ys += [high, high, low]
+                    rs += [r_high, r_low, r_high]
+                acc[...] += dot_t(jnp.concatenate(ys, axis=1), jnp.concatenate(rs, axis=1))
                 return carry
 
-            lax.fori_loop(0, w_dim, step, 0, unroll=2)
+            lax.fori_loop(0, w_dim // 2, step, 0)
             for s in range(phys):
                 w1[offset + t, :, s * bond:(s + 1) * bond] = acc[s * bond:(s + 1) * bond, :]
 
-        def stacked(y_high, y_low, t, w):
-            high = y_high[t, pl.ds(w * phys, phys)].reshape(phys * bond, bond)
-            low = y_low[t, pl.ds(w * phys, phys)].reshape(phys * bond, bond)
-            return jnp.concatenate([high, low, high], axis=0)
+        def stacked(y_high, y_low, t, i):
+            pair = []
+            for j in range(2):
+                at = pl.ds((2 * i + j) * phys, phys)
+                high = y_high[t, at].reshape(phys * bond, bond)
+                low = y_low[t, at].reshape(phys * bond, bond)
+                pair.append(jnp.concatenate([high, low, high], axis=0))
+            return jnp.concatenate(pair, axis=1)
 
         norm = epsilon + sum(total(v1[u] * v1[u]) for u in range(sectors)) / entries
         scale_split(v1, jnp.sqrt(norm))
         turn(v1, 0)
 
         env_copy[0].wait_send()
-        for copy in env_copy[1:]:
-            copy.start()
+        env_copy[1].start()
         w_copy = [remote(w1.at[offset + t], w1.at[offset + t], 1 + halves + t) for t in range(halves)]
         for t in range(halves):
             env_copy[t].wait_recv()
             contract(t, yh1, yl1)
             right(t)
+            if t + 1 < halves:
+                env_copy[t + 1].wait_send()
             w_copy[t].start()
-        for copy in env_copy[1:]:
-            copy.wait_send()
-
-        def grow_one(w, carry):
-            for t in range(halves):
-                g11[w, t] = dot(vt[t, :bond, :], stacked(yh1, yl1, t, w))
+
+        def grow_one(i, carry):
+            for t in range(halves):
+                out = dot(vt[t, :bond, :], stacked(yh1, yl1, t, i))
+                for j in range(2):
+                    g11[2 * i + j, t] = out[:, j * bond:(j + 1) * bond]
             return carry
 
-        lax.fori_loop(0, w_dim, grow_one, 0)
+        lax.fori_loop(0, w_dim // 2, grow_one, 0)
         for copy in w_copy:
             copy.wait()
 
@@ -181,25 +190,30 @@
 
         mine[...] = jnp.zeros_like(mine)
 
-        def grow_two(w, carry):
-            for t in range(halves):
-                out = dot(vt[t], stacked(yh2, yl2, t, w))
-                gx[w, t] = out[:bond]
-                g22[w, t] = out[bond:]
-                prod = out[bond:] * lr[1, t, w]
-                mine[...] += jnp.sum(prod.reshape(bond // 8, 8, bond), axis=0)
+        def grow_two(i, carry):
+            for t in range(halves):
+                out = dot(vt[t], stacked(yh2, yl2, t, i))
+                for j in range(2):
+                    w = 2 * i + j
+                    gx[w, t] = out[:bond, j * bond:(j + 1) * bond]
+                    part = out[bond:, j * bond:(j + 1) * bond]
+                    g22[w, t] = part
+                    prod = part * lr[1, t, w]
+                    mine[...] += jnp.sum(prod.reshape(bond // 8, 8, bond), axis=0)
             return carry
 
-        lax.fori_loop(0, w_dim, grow_two, 0)
+        lax.fori_loop(0, w_dim // 2, grow_two, 0)
         r_copy = remote(mine, theirs, 1 + 2 * halves)
         r_copy.start()
 
-        def grow_three(w, carry):
-            for t in range(halves):
-                gx[w, t] += dot(vt[t, bond:, :], stacked(yh1, yl1, t, w))
+        def grow_three(i, carry):
+            for t in range(halves):
+                out = dot(vt[t, bond:, :], stacked(yh1, yl1, t, i))
+                for j in range(2):
+                    gx[2 * i + j, t] += out[:, j * bond:(j + 1) * bond]
             return carry
 
-        lax.fori_loop(0, w_dim, grow_three, 0)
+        lax.fori_loop(0, w_dim // 2, grow_three, 0)
         r_copy.wait()
         r2 = total(mine[...] + theirs[...]) / entries
         g = 0.5 * (r1 - r2)
@@ -225,6 +239,22 @@
         lax.fori_loop(0, w_dim, finish, 0)
 
     return kernel
+
+
+def place(fresh, grown, energy, fresh_out, grown_out, energy_out, fresh_buf, grown_buf, sems, out_sems):
+    w_dim = grown.shape[0]
+    parts = [(grown.at[pl.ds(i, 2)], grown_buf.at[pl.ds(i, 2)], grown_out.at[pl.ds(i, 2)]) for i in range(0, w_dim, 2)]
+    parts.append((fresh, fresh_buf, fresh_out))
+    ins = [pltpu.make_async_copy(src, buf, sems.at[i]) for i, (src, buf, _) in enumerate(parts)]
+    outs = [pltpu.make_async_copy(buf, dst, out_sems.at[i]) for i, (_, buf, dst) in enumerate(parts)]
+    for copy in ins:
+        copy.start()
+    energy_out[...] = energy[...]
+    for copy, after in zip(ins, outs):
+        copy.wait()
+        after.start()
+    for copy in outs:
+        copy.wait()
 
 
 def shards(edge_env, start_vector, mpo, sector_map):
@@ -245,7 +275,7 @@
         out_shape=(
             jax.ShapeDtypeStruct((halves, bond, phys * bond), f32),
             jax.ShapeDtypeStruct(env, f32),
-            jax.ShapeDtypeStruct((8, 128), f32),
+            jax.ShapeDtypeStruct((1, 1), f32),
         ),
         in_specs=[hbm, hbm, vmem, smem],
         out_specs=(vmem, vmem, vmem),
@@ -274,8 +304,20 @@
         ],
         compiler_params=pltpu.CompilerParams(
             collective_id=0, has_side_effects=True, vmem_limit_bytes=56 * 1024 * 1024),
-    )(edge_env[0], start_vector[0], mpo, sector_map)
-    return (fresh[None], grown[None], energy[0, :1])
+    )(edge_env[0], start_vector[0], mpo, sector_map.T)
+    fresh, grown, energy = pl.pallas_call(
+        place,
+        out_shape=tuple(jax.ShapeDtypeStruct(value.shape, f32) for value in (fresh, grown, energy)),
+        in_specs=[hbm, hbm, vmem],
+        out_specs=(hbm, hbm, vmem),
+        scratch_shapes=[
+            pltpu.VMEM(fresh.shape, f32),
+            pltpu.VMEM(grown.shape, f32),
+            pltpu.SemaphoreType.DMA((w_dim // 2 + 1,)),
+            pltpu.SemaphoreType.DMA((w_dim // 2 + 1,)),
+        ],
+    )(fresh, grown, energy)
+    return (fresh[None], grown[None], energy.reshape(1))
 
 
 def solution(mesh):

time: 167 us -> 155 us (0.928)
  local copies, waits for them, and re-layouts: 7.34 us -> 0 us
  Pallas kernels: 159 us -> 154 us
    pallas_call x1, Pallas kernels: 159 us -> 150 us  [shards(): pl.pallas_call(make_kernel(seg_count, w_dim, sectors, bond, phys), out_sh...]
    unnamed x3 -> x0, local copies, waits for them, and re-layouts: 6.16 us -> none
    pallas_call x0 -> x1, Pallas kernels: none -> 3.73 us  [shards(): pl.pallas_call(place, out_shape=tuple((jax.ShapeDtypeStruct(value.shape,...]
where the time goes in v1:
time: 155 us
  Pallas kernels  154 us (99%)
    pallas_call x1, Pallas kernels, shards(): pl.pallas_call(make_kernel(seg_count, w_dim, sectors, bond, phys), out_sh...  150 us
    pallas_call x1, Pallas kernels, shards(): pl.pallas_call(place, out_shape=tuple((jax.ShapeDtypeStruct(value.shape,...  3.73 us

profile of v1, /device:TPU:8, one launch (start us, length us, event | category | flops | bytes accessed | tf_op | source)
XLA Modules:
  0.0 154.8 jit_solution(182673214384169563)
XLA Ops:
  0.6 150.4 %shard_map.67 = (f32[2,128,512]{2,1,0:T(8,128)}, f32[14,2,128,128]{3,2,1,0:T(8,128)}, f32[1,1]{1,0:T(1,128)}) custom-call(f32[14,4,128,128]{3,2,1,0:T(8,128)} %bitcast.6, f32[2,128,512]{2,1,0:T(8,128)} %bitcast.7, f32[56,56]{1,0:T(8,128)} %mpo.1, s32[4,14]{1,0:T(4,128)} %bitcast.8), custom_call_target="tpu_custom_call" | custom-call | tf_op jit(solution)/shard_map/pallas_call | solution.py:273
  151.1 3.7 %shard_map.68 = (f32[2,128,512]{2,1,0:T(8,128)}, f32[14,2,128,128]{3,2,1,0:T(8,128)}, f32[1,1]{1,0:T(1,128)}) custom-call(f32[2,128,512]{2,1,0:T(8,128)} %get-tuple-element.9.fresh, f32[14,2,128,128]{3,2,1,0:T(8,128)} %get-tuple-element.10.grown, f32[1,1]{1,0:T(1,128)} %get-tuple-element.11.energy), custom_call_target="tpu_custom_call" | custom-call | tf_op jit(solution)/shard_map/pallas_call | solution.py:308

commit v2 on v1

--- a/solution.py
+++ b/solution.py
@@ -53,7 +53,9 @@
                 device_id=peer, device_id_type=pl.DeviceIdType.MESH)
 
         vec_copy = remote(start, v1.at[pl.ds(offset, halves)], 0)
-        env_copy = [remote(env.at[:, halves - offset + t], lr.at[upper, t], 1 + t) for t in range(halves)]
+        env_copy = [remote(env.at[cut, halves - offset + t], lr.at[upper, t, cut], i)
+                    for i, t, cut in ((1, 0, pl.ds(0, w_dim // 2)), (2, 0, pl.ds(w_dim // 2, w_dim // 2)),
+                                      (3, 1, pl.ds(0, w_dim)))]
         own_vec = pltpu.make_async_copy(start, v1.at[pl.ds(offset, halves)], local.at[0])
         own_env = [pltpu.make_async_copy(env.at[:, offset + t], lr.at[upper, t], local.at[1 + t]) for t in range(halves)]
         vec_copy.start()
@@ -75,6 +77,7 @@
         for copy in own_env:
             copy.wait()
         vec_copy.wait()
+        env_copy[1].start()
 
         def scale_split(ref, divisor):
             for u in range(sectors):
@@ -155,14 +158,16 @@
         turn(v1, 0)
 
         env_copy[0].wait_send()
-        env_copy[1].start()
-        w_copy = [remote(w1.at[offset + t], w1.at[offset + t], 1 + halves + t) for t in range(halves)]
+        env_copy[2].start()
+        env_copy[1].wait_send()
+        w_copy = [remote(w1.at[offset + t], w1.at[offset + t], 2 + halves + t) for t in range(halves)]
         for t in range(halves):
-            env_copy[t].wait_recv()
+            for copy in (env_copy[:2], env_copy[2:])[t]:
+                copy.wait_recv()
             contract(t, yh1, yl1)
             right(t)
             if t + 1 < halves:
-                env_copy[t + 1].wait_send()
+                env_copy[2].wait_send()
             w_copy[t].start()
 
         def grow_one(i, carry):
@@ -202,8 +207,8 @@
                     mine[...] += jnp.sum(prod.reshape(bond // 8, 8, bond), axis=0)
             return carry
 
-        lax.fori_loop(0, w_dim // 2, grow_two, 0)
-        r_copy = remote(mine, theirs, 1 + 2 * halves)
+        lax.fori_loop(0, w_dim // 2, grow_two, 0, unroll=7)
+        r_copy = remote(mine, theirs, 2 + 2 * halves)
         r_copy.start()
 
         def grow_three(i, carry):
@@ -236,7 +241,7 @@
                 grown_out[w, t] = c11 * g11[w, t] + c12 * gx[w, t] + c22 * g22[w, t]
             return carry
 
-        lax.fori_loop(0, w_dim, finish, 0)
+        lax.fori_loop(0, w_dim, finish, 0, unroll=7)
 
     return kernel
 
@@ -298,8 +303,8 @@
             pltpu.VMEM(env, f32),
             pltpu.VMEM((8, 128), f32),
             pltpu.VMEM((8, 128), f32),
-            pltpu.SemaphoreType.DMA((2 + 2 * halves,)),
-            pltpu.SemaphoreType.DMA((2 + 2 * halves,)),
+            pltpu.SemaphoreType.DMA((3 + 2 * halves,)),
+            pltpu.SemaphoreType.DMA((3 + 2 * halves,)),
             pltpu.SemaphoreType.DMA((1 + halves,)),
         ],
         compiler_params=pltpu.CompilerParams(

time: 155 us -> 154 us (level)
  no operation moved by 1% of the time
where the time goes in v2:
time: 154 us
  Pallas kernels  154 us (100%)
    pallas_call x1, Pallas kernels, shards(): pl.pallas_call(make_kernel(seg_count, w_dim, sectors, bond, phys), out_sh...  150 us
    pallas_call x1, Pallas kernels, shards(): pl.pallas_call(place, out_shape=tuple((jax.ShapeDtypeStruct(value.shape,...  3.73 us

profile of v2, /device:TPU:8, one launch (start us, length us, event | category | flops | bytes accessed | tf_op | source)
XLA Modules:
  0.0 154.2 jit_solution(3101048767560366090)
XLA Ops:
  0.6 149.8 %shard_map.67 = (f32[2,128,512]{2,1,0:T(8,128)}, f32[14,2,128,128]{3,2,1,0:T(8,128)}, f32[1,1]{1,0:T(1,128)}) custom-call(f32[14,4,128,128]{3,2,1,0:T(8,128)} %bitcast.6, f32[2,128,512]{2,1,0:T(8,128)} %bitcast.7, f32[56,56]{1,0:T(8,128)} %mpo.1, s32[4,14]{1,0:T(4,128)} %bitcast.8), custom_call_target="tpu_custom_call" | custom-call | tf_op jit(solution)/shard_map/pallas_call | solution.py:278
  150.5 3.7 %shard_map.68 = (f32[2,128,512]{2,1,0:T(8,128)}, f32[14,2,128,128]{3,2,1,0:T(8,128)}, f32[1,1]{1,0:T(1,128)}) custom-call(f32[2,128,512]{2,1,0:T(8,128)} %get-tuple-element.9.fresh, f32[14,2,128,128]{3,2,1,0:T(8,128)} %get-tuple-element.10.grown, f32[1,1]{1,0:T(1,128)} %get-tuple-element.11.energy), custom_call_target="tpu_custom_call" | custom-call | tf_op jit(solution)/shard_map/pallas_call | solution.py:313
